TPU v7x, 512 devices: a whole 4x8x8 slice. The times are simulated.
512 devices in a mesh: section: 32 (over y, x_lo, core), dp: 16 (over z, x_hi).
Axes of the slice: x: 4 (x_hi: 2, x_lo: 2; x = x_hi * 2 + x_lo), y: 8, z: 8, core: 2. Of those that a mesh axis runs over, the one named last changes fastest.
Arguments:
- queries: bfloat16 [32, 2048, 2048], P('section', 'dp'), may hold values from -200 to 200, as said below
- key_values: bfloat16 [32, 1024, 4096], P('section', 'dp'), may hold values from -8 to 8, as said below
- d_context: bfloat16 [32, 2048, 2048], P('section', 'dp'), may hold values from -6 to 6
- w_kv: bfloat16 [32, 4096, 4096], P('section', 'dp'), may hold values from -0.09375 to 0.09375
- enc_len: int32 [16], P('dp'), may hold values from 32 to 64
Outputs:
- query_grads: bfloat16 [32, 2048, 2048], P('section', 'dp')
- encoder_grad: float32 [1024, 4096], P('section', 'dp')
Inputs may be any that keep to these rules, and one draw needn't show every extreme that they name: queries: entries stay within the range. `key_values`: entries stay within the range.
All inputs are finite; a program needn't handle non-finite values.
Results may differ from a plain program's by a relative error of at most 0.0074.
Values may be sent and summed in bfloat16 or wider, within the bound.
A program may use at most 64 MiB of HBM per device.

v0:
```python
import jax
import jax.numpy as jnp
from jax import lax
from jax.sharding import PartitionSpec as P

HEADS = 8
HEAD_DIM = 256
TDEC = 128
SENC = 64


def attend_back(queries, key_values, d_context, enc_len):
    width = HEADS * HEAD_DIM
    micro = queries.shape[0] // TDEC
    scale = HEAD_DIM ** (-0.5)
    qfull = queries.reshape(micro, TDEC, HEADS, HEAD_DIM)
    kfull = key_values[:, :width].reshape(micro, SENC, HEADS, HEAD_DIM)
    vfull = key_values[:, width:].reshape(micro, SENC, HEADS, HEAD_DIM)
    dfull = d_context.reshape(micro, TDEC, HEADS, HEAD_DIM)
    scores = jnp.einsum("mthe,mshe->mhts", qfull, kfull, preferred_element_type=jnp.float32) * scale
    places = jnp.arange(SENC, dtype=jnp.int32)
    live = places[None, None, None, :] < enc_len[:, None, None, None]
    scores = jnp.where(live, scores, -1000000000.0)
    peak = jnp.max(scores, axis=-1, keepdims=True)
    expo = jnp.exp(scores - peak)
    probs = expo / jnp.sum(expo, axis=-1, keepdims=True)
    probs_low = probs.astype(jnp.bfloat16)
    context = jnp.einsum("mhts,mshe->mthe", probs_low, vfull, preferred_element_type=jnp.float32)
    delta = jnp.sum(dfull.astype(jnp.float32) * context, axis=-1)
    delta = jnp.transpose(delta, (0, 2, 1))[..., None]
    dprobs = jnp.einsum("mthe,mshe->mhts", dfull, vfull, preferred_element_type=jnp.float32)
    dscores = (probs * (dprobs - delta)).astype(jnp.bfloat16)
    dquery = (
        jnp.einsum("mhts,mshe->mthe", dscores, kfull, preferred_element_type=jnp.float32) * scale
    ).astype(jnp.bfloat16)
    dkey = (
        jnp.einsum("mhts,mthe->mshe", dscores, qfull, preferred_element_type=jnp.float32) * scale
    ).astype(jnp.bfloat16)
    dvalue = jnp.einsum(
        "mhts,mthe->mshe", probs_low, dfull, preferred_element_type=jnp.float32
    ).astype(jnp.bfloat16)
    dquery = dquery.reshape(micro * TDEC, width)
    dkey = dkey.reshape(micro * SENC, width)
    dvalue = dvalue.reshape(micro * SENC, width)
    return (dquery, dkey, dvalue)


def project_rows(piece, weights):
    return lax.dot_general(
        piece, weights, (((1,), (1,)), ((), ())), preferred_element_type=jnp.float32
    )


def local(queries, key_values, d_context, w_kv, enc_len):
    dquery, dkey, dvalue = attend_back(queries[0], key_values[0], d_context[0], enc_len)
    weights = w_kv[0]
    kv_grads = jnp.concatenate([dkey, dvalue], axis=1)
    partial_sum = project_rows(lax.all_gather(kv_grads, "dp", axis=0, tiled=True), weights)
    total = lax.psum(partial_sum, "section")
    block = partial_sum.shape[0] // lax.axis_size("section")
    encoder_grad = lax.dynamic_slice_in_dim(total, lax.axis_index("section") * block, block, 0)
    return (dquery[None], encoder_grad)


def solution(mesh):
    in_specs = (
        P("section", "dp", None),
        P("section", "dp", None),
        P("section", "dp", None),
        P("section", "dp", None),
        P("dp"),
    )
    out_specs = (P("section", "dp", None), P("section", "dp"))
    return jax.shard_map(local, mesh=mesh, in_specs=in_specs, out_specs=out_specs, check_vma=False)
```

profile of v0, /device:TPU:1, one launch (start us, length us, event | category | flops | bytes accessed | tf_op | source)
XLA Modules:
  0.0 414.8 jit_solution(11439092125225520889)
XLA Ops:
  7.2 0.0 all-gather.2.cloned.1.call-start
  7.2 1.9 fusion.30
  9.1 1.1 copy.27
  11.0 0.3 fusion.12
  11.3 0.7 copy-done.1
  12.0 0.8 fusion.31
  12.8 1.3 copy.15
  14.1 1.2 copy.17
  15.3 1.1 copy.28
  16.5 2.0 fusion.32
  18.5 1.9 fusion.5
  20.4 1.3 fusion.14
  21.7 0.2 fusion.37
  22.0 1.0 copy.30
  23.0 0.8 pad_maximum_fusion
  23.8 0.0 all-gather.2.cloned.1.call-update
  23.8 0.0 all-reduce.2.cloned.1.call-start
  23.9 147.1 %all-gather.2.cloned.1.call-done = bf16[1024,4096]{1,0:T(8,128)(2,1)} async-done(((bf16[64,4096]{1,0:T(8,128)(2,1)}), bf16[1024,4096]{1,0:T(8,128)(2,1)}) %all-gather.2.cloned.1.call-update) | async-done | bytes 8388624 | tf_op jit(solution)/shard_map/all_gather | solution.py:58
  170.9 6.8 %fusion.1 = f32[1024,256]{1,0:T(8,128)} fusion(bf16[1024,4096]{1,0:T(8,128)(2,1)} %all-gather.2.cloned.1.call-done, bf16[1,256,4096]{2,1,0:T(8,128)(2,1)S(1)} %copy-done), kind=kOutput, calls=%fused_computation.1 | convolution fusion | flops 2147483648 | bytes 11534336 | tf_op jit(solution)/shard_map/dot_general | solution.py:49
  177.8 0.3 fusion.6
  178.1 0.3 copy.19
  178.4 1.0 copy.24
  179.4 227.1 %all-reduce.2.cloned.1.call-done = f32[1024,256]{1,0:T(8,128)} async-done(((f32[1024,256]{1,0:T(8,128)}), f32[1024,256]{1,0:T(8,128)}) %all-reduce.2.cloned.1.call-update) | async-done | bytes 1048592 | tf_op jit(solution)/shard_map/psum | solution.py:59
  406.6 1.4 constant_dynamic-slice_fusion
  (6 shorter events, 0.1 us)
Async XLA Ops:
  7.2 163.8 %copy-start = (bf16[1,256,4096]{2,1,0:T(8,128)(2,1)S(1)}, bf16[1,256,4096]{2,1,0:T(8,128)(2,1)}, u32[]{:S(2)}) copy-start(bf16[1,256,4096]{2,1,0:T(8,128)(2,1)} %param.8) | copy-start | bytes 6291460
  7.2 163.8 %all-gather.2.cloned.1.call-start = ((), (), s32[]{:S(2)}) async-start(), calls=%async_computation | async-start | bytes 8912896 | tf_op jit(solution)/shard_map/all_gather | solution.py:58
  11.3 0.7 copy-start.1
  23.8 382.7 %all-reduce.2.cloned.1.call-start = ((), (), s32[]{:S(2)}) async-start(), calls=%async_computation.1 | async-start | bytes 2097152 | tf_op jit(solution)/shard_map/psum | solution.py:59
Sparse Core Ops, SparseCore 0:
  23.9 146.9 all-gather.1
  177.9 228.6 all-reduce.1
where the time goes:
time: 415 us
  waiting for transfers between devices  374 us (90%)
  between operations  14.8 us (4%)
  matrix products  13 us (3%)
  local copies, waits for them, and re-layouts  11.1 us (3%)
    psum x1, waiting for transfers between devices, local(): total = lax.psum(partial_sum, 'section')  227 us
    all_gather x1, waiting for transfers between devices, local(): lax.all_gather(kv_grads, 'dp', axis=0, tiled=True)  147 us
  transfers between devices with their start and end apart: 2, of which 2 were waited for; matrix products, arithmetic and copies ran while one was open for 0% of the time, Pallas kernels for 0%

commit v1 on v0

v1 whole, which is shorter than its diff:
```python
import functools

import jax
import jax.numpy as jnp
from jax import lax
from jax.experimental import pallas as pl
from jax.experimental.pallas import tpu as pltpu
from jax.sharding import PartitionSpec as P

MESH = pl.DeviceIdType.MESH
BF = jnp.bfloat16
F32 = jnp.float32
HEADS = 8
HALF = HEADS // 2
HD = 256
TDEC = 128
SENC = 64
WIDTH = HEADS * HD
RING = 8
SCALE = HD ** (-0.5)


def dot_nt(a, b):
    return lax.dot_general(a, b, (((1,), (1,)), ((), ())), preferred_element_type=F32)


def dot_nn(a, b):
    return lax.dot_general(a, b, (((1,), (0,)), ((), ())), preferred_element_type=F32)


def dot_tn(a, b):
    return lax.dot_general(a, b, (((0,), (0,)), ((), ())), preferred_element_type=F32)


def kernel(
    len_ref, q_ref, kv_ref, do_ref, w_ref, dq_ref, eg_ref,
    g, xs, wv, asend, abuf, bsend, bbuf,
    wl_sem, ws_sem, wr_sem, xs_sem, xr_sem, zs_sem, zr_sem, as_sem, ar_sem, bs_sem, br_sem,
):
    section, dp = lax.axis_index("section"), lax.axis_index("dp")
    y, xl, c = section // 4, (section // 2) % 2, section % 2
    z, xh = dp // 2, dp % 2

    def device(y, xl, c, z, xh):
        return (y * 4 + xl * 2 + c, z * 2 + xh)

    def around(k):
        return device(y, (xl + k // 4) % 2, (c + (k // 2) % 2) % 2, z, (xh + k % 2) % 2)

    barrier = pltpu.get_barrier_semaphore()
    for up in (1, RING - 1):
        pl.semaphore_signal(barrier, inc=1, device_id=device(y, xl, c, (z + up) % RING, xh), device_id_type=MESH)
    for k in range(1, 8):
        pl.semaphore_signal(barrier, inc=1, device_id=around(k), device_id_type=MESH)
        pl.semaphore_signal(barrier, inc=1, device_id=device((y + k) % RING, xl, c, z, xh), device_id_type=MESH)

    def w_columns(half, hh, part):
        return pl.ds(pl.multiple_of(part * WIDTH + (half * HALF + hh) * HD, HD), HD)

    def w_local(hh, part):
        return pltpu.make_async_copy(
            w_ref.at[:, w_columns(xh, hh, part)],
            wv.at[hh, pl.ds(0, HD), pl.ds(part * HD, HD)],
            wl_sem.at[hh, part],
        )

    def w_remote(hh, part):
        return pltpu.make_async_remote_copy(
            src_ref=w_ref.at[:, w_columns(1 - xh, hh, part)],
            dst_ref=wv.at[hh, pl.ds(HD, HD), pl.ds(part * HD, HD)],
            send_sem=ws_sem.at[hh, part],
            recv_sem=wr_sem.at[hh, part],
            device_id=around(1),
            device_id_type=MESH,
        )

    for hh in range(HALF):
        for part in range(2):
            w_local(hh, part).start()

    def x_copy(hh):
        return pltpu.make_async_remote_copy(
            src_ref=xs.at[hh],
            dst_ref=g.at[0, hh, pl.ds(SENC, SENC)],
            send_sem=xs_sem.at[hh],
            recv_sem=xr_sem.at[hh],
            device_id=around(1),
            device_id_type=MESH,
        )

    def z_copy(s, d, r, hh):
        source = g.at[0, hh, pl.ds(r * SENC, SENC)] if s == 1 else g.at[2 * s - 3 + r, hh, pl.ds(d * SENC, SENC)]
        place = g.at[7, hh, pl.ds(r * SENC, SENC)] if s == 4 else g.at[2 * s - 1 + r, hh, pl.ds(d * SENC, SENC)]
        return pltpu.make_async_remote_copy(
            src_ref=source,
            dst_ref=place,
            send_sem=zs_sem.at[s - 1, d, r, hh],
            recv_sem=zr_sem.at[s - 1, d, r, hh],
            device_id=device(y, xl, c, (z + (1 if d == 0 else RING - 1)) % RING, xh),
            device_id_type=MESH,
        )

    live = lax.broadcasted_iota(jnp.int32, (SENC, TDEC), 0) < len_ref[0]

    def head(index):
        cols = pl.ds(pl.multiple_of(index * HD, HD), HD)
        vcols = pl.ds(pl.multiple_of(WIDTH + index * HD, HD), HD)
        q, k, v, do = q_ref[:, cols], kv_ref[:, cols], kv_ref[:, vcols], do_ref[:, cols]
        scores = jnp.where(live, dot_nt(k, q) * SCALE, -1e9)
        expo = jnp.exp(scores - jnp.max(scores, axis=0, keepdims=True))
        probs = expo / jnp.sum(expo, axis=0, keepdims=True)
        probs_low = probs.astype(BF)
        dprobs = dot_nt(v, do)
        delta = jnp.sum(probs_low.astype(F32) * dprobs, axis=0, keepdims=True)
        dscores = (probs * (dprobs - delta)).astype(BF)
        dq_ref[:, cols] = (dot_tn(dscores, k) * SCALE).astype(BF)
        dk = (dot_nn(dscores, q) * SCALE).astype(BF)
        dv = dot_nn(probs_low, do).astype(BF)
        return dk, dv

    def pair(hh):
        dk, dv = head(xh * HALF + hh)
        g[0, hh, :SENC, :HD] = dk
        g[0, hh, :SENC, HD:] = dv
        dk, dv = head((1 - xh) * HALF + hh)
        xs[hh, :, :HD] = dk
        xs[hh, :, HD:] = dv

    def send_pair(hh):
        z_copy(1, 0, 0, hh).start()
        z_copy(1, 1, 0, hh).start()
        x_copy(hh).start()

    pair(0)
    pl.semaphore_wait(barrier, 16)
    send_pair(0)

    def more(hh, _):
        pair(hh)
        send_pair(hh)
        return 0

    lax.fori_loop(1, HALF, more, 0)

    for hh in range(HALF):
        for part in range(2):
            w_remote(hh, part).start()

    def from_partner(hh, _):
        x_copy(hh).wait_recv()
        z_copy(1, 0, 1, hh).start()
        z_copy(1, 1, 1, hh).start()
        return 0

    lax.fori_loop(0, HALF, from_partner, 0)

    def pass_on(s, r, hh):
        z_copy(s, 0, r, hh).wait_recv()
        if s < 3 or r == 0:
            z_copy(s + 1, 0, r, hh).start()
        z_copy(s, 1, r, hh).wait_recv()
        if s < 3 or r == 1:
            z_copy(s + 1, 1, r, hh).start()

    for s in (1, 2):
        for r in (0, 1):
            lax.fori_loop(0, HALF, lambda hh, _, s=s, r=r: (pass_on(s, r, hh), 0)[1], 0)

    for hh in range(HALF):
        for part in range(2):
            w_local(hh, part).wait()
            w_remote(hh, part).wait_recv()

    def product(t):
        total = dot_nt(g[t, 0], wv[0])
        for hh in range(1, HALF):
            total += dot_nt(g[t, hh], wv[hh])
        return total.astype(BF)

    def product_ring(t):
        total = product(t)
        group, r = (t + 1) // 2, (t + 1) % 2
        for d in range(2):
            for j in range(2):
                for n in range(2):
                    at = d * 64 + j * 32
                    asend[group, r * 4 + j * 2 + n, d * 32 : d * 32 + 32, :] = total[at : at + 32, n * HD : n * HD + HD]

    def product_edge(t, group):
        total = product(t)
        for r in range(2):
            for j in range(2):
                for n in range(2):
                    at = r * 64 + j * 32
                    asend[group, r * 4 + j * 2 + n, :32, :] = total[at : at + 32, n * HD : n * HD + HD]

    def a_piece(k):
        return ((xl + k // 4 + xh) % 2) * 4 + ((c + (k // 2) % 2) % 2) * 2 + k % 2

    def a_copy(group, k):
        rows = pl.ds(0, 32 if group in (0, 4) else 64)
        return pltpu.make_async_remote_copy(
            src_ref=asend.at[group, a_piece(k), rows],
            dst_ref=abuf.at[group, k, rows],
            send_sem=as_sem.at[group, k],
            recv_sem=ar_sem.at[group, k],
            device_id=around(k),
            device_id_type=MESH,
        )

    def a_start(group):
        for k in range(1, 8):
            a_copy(group, k).start()

    def b_place(group, d):
        return (z + (group if d == 1 else RING - group)) % RING

    def b_copy(group, d):
        return pltpu.make_async_remote_copy(
            src_ref=bsend.at[group, pl.ds(d * 32, 32)],
            dst_ref=bbuf.at[y],
            send_sem=bs_sem.at[group, d],
            recv_sem=br_sem.at[y],
            device_id=device(b_place(group, d), xl, c, z, xh),
            device_id_type=MESH,
        )

    def gather_sum(group):
        rows = 32 if group in (0, 4) else 64
        total = asend[group, a_piece(0), :rows, :].astype(F32)
        for k in range(1, 8):
            a_copy(group, k).wait_recv()
            total += abuf[group, k, :rows, :].astype(F32)
        bsend[group, :rows, :] = total
        for d in range(rows // 32):
            away = b_place(group, d) != y

            @pl.when(away)
            def _():
                b_copy(group, d).start()

            @pl.when(jnp.logical_not(away))
            def _():
                bbuf[y] = total[d * 32 : d * 32 + 32]

    def last_hop(r, hh):
        pass_on(3, r, hh)

    def step_a(hh, _):
        last_hop(0, hh)
        product_ring(1 + hh)
        return 0

    lax.fori_loop(0, 2, step_a, 0)
    a_start(1)
    lax.fori_loop(2, 4, step_a, 0)
    a_start(2)
    last_hop(1, 0)
    product_edge(0, 0)
    a_start(0)
    last_hop(1, 1)
    product_ring(5)
    last_hop(1, 2)
    gather_sum(1)
    last_hop(1, 3)
    product_ring(6)
    a_start(3)
    gather_sum(2)
    gather_sum(0)

    for r in range(2):
        lax.fori_loop(0, HALF, lambda hh, _, r=r: (z_copy(4, r, r, hh).wait_recv(), 0)[1], 0)
    product_edge(7, 4)
    a_start(4)
    gather_sum(3)
    gather_sum(4)

    for hh in range(HALF):
        x_copy(hh).wait_send()
        for part in range(2):
            w_remote(hh, part).wait_send()

    def sent(hh, _):
        for s in (1, 2, 3):
            for d in range(2):
                for r in range(2):
                    z_copy(s, d, r, hh).wait_send()
        for r in range(2):
            z_copy(4, r, r, hh).wait_send()
        return 0

    lax.fori_loop(0, HALF, sent, 0)
    for group in range(5):
        for k in range(1, 8):
            a_copy(group, k).wait_send()
        for d in range(1 if group in (0, 4) else 2):

            @pl.when(b_place(group, d) != y)
            def _():
                b_copy(group, d).wait_send()

    for k in range(1, RING):
        other = (y + k) % RING
        pltpu.make_async_remote_copy(
            src_ref=bsend.at[0, pl.ds(0, 32)],
            dst_ref=bbuf.at[other],
            send_sem=bs_sem.at[0, 0],
            recv_sem=br_sem.at[other],
            device_id=device(other, xl, c, z, xh),
            device_id_type=MESH,
        ).wait_recv()
    total = bbuf[0]
    for k in range(1, RING):
        total += bbuf[k]
    eg_ref[...] = total


def local(queries, key_values, d_context, w_kv, enc_len):
    vmem = pl.BlockSpec(memory_space=pltpu.VMEM)
    dma = pltpu.SemaphoreType.DMA
    dquery, encoder_grad = pl.pallas_call(
        kernel,
        out_shape=(
            jax.ShapeDtypeStruct((TDEC, WIDTH), BF),
            jax.ShapeDtypeStruct((32, HD), F32),
        ),
        in_specs=[pl.BlockSpec(memory_space=pltpu.SMEM), vmem, vmem, vmem, pl.BlockSpec(memory_space=pl.ANY)],
        out_specs=(vmem, vmem),
        scratch_shapes=[
            pltpu.VMEM((8, HALF, 2 * SENC, 2 * HD), BF),
            pltpu.VMEM((HALF, SENC, 2 * HD), BF),
            pltpu.VMEM((HALF, 2 * HD, 2 * HD), BF),
            pltpu.VMEM((5, 8, 64, HD), BF),
            pltpu.VMEM((5, 8, 64, HD), BF),
            pltpu.VMEM((5, 64, HD), F32),
            pltpu.VMEM((RING, 32, HD), F32),
            dma((HALF, 2)), dma((HALF, 2)), dma((HALF, 2)),
            dma((HALF,)), dma((HALF,)),
            dma((4, 2, 2, HALF)), dma((4, 2, 2, HALF)),
            dma((5, 8)), dma((5, 8)),
            dma((5, 2)), dma((RING,)),
        ],
        compiler_params=pltpu.CompilerParams(
            collective_id=0, has_side_effects=True, vmem_limit_bytes=40 * 1024 * 1024
        ),
    )(enc_len, queries[0], key_values[0], d_context[0], w_kv[0])
    return dquery[None], encoder_grad


def solution(mesh):
    in_specs = (
        P("section", "dp", None),
        P("section", "dp", None),
        P("section", "dp", None),
        P("section", "dp", None),
        P("dp"),
    )
    out_specs = (P("section", "dp", None), P("section", "dp"))
    return jax.shard_map(local, mesh=mesh, in_specs=in_specs, out_specs=out_specs, check_vma=False)
```

time: 415 us -> 73.6 us (0.18)
  waiting for transfers between devices: 374 us -> 0 us
  Pallas kernels: 0 us -> 65.5 us
  between operations: 14.8 us -> 1.3 us
  matrix products: 13 us -> 0 us
  local copies, waits for them, and re-layouts: 11.1 us -> 6.12 us
    psum x1 -> x0, waiting for transfers between devices: 227 us -> none  [local(): total = lax.psum(partial_sum, 'section')]
    all_gather x1 -> x0, waiting for transfers between devices: 147 us -> none  [local(): lax.all_gather(kv_grads, 'dp', axis=0, tiled=True)]
    pallas_call x0 -> x1, Pallas kernels: none -> 65.5 us  [local(): pl.pallas_call(kernel, out_shape=(jax.ShapeDtypeStruct((TDEC, WIDTH), BF)...]
    dot_general x7 -> x0, matrix products: 13 us -> none  [the longest x1 6.82 us: project_rows(): lax.dot_general(piece, weights, (((1,), (1,)), ((), ())), preferred_eleme...]
  transfers between devices with their start and end apart: 2 -> 0, of which waited for: 2 -> 0; matrix products, arithmetic and copies ran while one was open for 0% -> 0% of each run, Pallas kernels for 0% -> 0%
where the time goes in v1:
time: 73.6 us; the launch traced here: 72.9 us
  Pallas kernels  65.5 us (89%)
  local copies, waits for them, and re-layouts  6.12 us (8%)
  between operations  1.3 us (2%)
    pallas_call x1, Pallas kernels, local(): pl.pallas_call(kernel, out_shape=(jax.ShapeDtypeStruct((TDEC, WIDTH), BF)...  65.5 us
    unnamed x10, local copies, waits for them, and re-layouts  6.12 us

profile of v1, /device:TPU:1, one launch (start us, length us, event | category | flops | bytes accessed | tf_op | source)
XLA Modules:
  0.0 72.9 jit_solution(17319943963337038147)
XLA Ops:
  1.3 0.0 copy-start
  1.3 1.6 %copy-done = bf16[1,256,4096]{2,1,0:T(8,128)(2,1)S(1)} copy-done((bf16[1,256,4096]{2,1,0:T(8,128)(2,1)S(1)}, bf16[1,256,4096]{2,1,0:T(8,128)(2,1)}, u32[]{:S(2)}) %copy-start) | copy-done | bytes 2097176
  2.9 0.0 copy-start.1
  2.9 1.0 %copy-done.1 = bf16[1,128,2048]{2,1,0:T(8,128)(2,1)S(1)} copy-done((bf16[1,128,2048]{2,1,0:T(8,128)(2,1)S(1)}, bf16[1,128,2048]{2,1,0:T(8,128)(2,1)}, u32[]{:S(2)}) %copy-start.1) | copy-done | bytes 524312
  3.9 0.0 copy-start.2
  3.9 1.0 %copy-done.2 = bf16[1,64,4096]{2,1,0:T(8,128)(2,1)S(1)} copy-done((bf16[1,64,4096]{2,1,0:T(8,128)(2,1)S(1)}, bf16[1,64,4096]{2,1,0:T(8,128)(2,1)}, u32[]{:S(2)}) %copy-start.2) | copy-done | bytes 524312
  5.0 0.0 copy-start.3
  5.0 1.0 %copy-done.3 = bf16[1,128,2048]{2,1,0:T(8,128)(2,1)S(1)} copy-done((bf16[1,128,2048]{2,1,0:T(8,128)(2,1)S(1)}, bf16[1,128,2048]{2,1,0:T(8,128)(2,1)}, u32[]{:S(2)}) %copy-start.3) | copy-done | bytes 524312
  6.0 65.5 %shard_map.68 = (bf16[128,2048]{1,0:T(8,128)(2,1)S(1)}, f32[32,256]{1,0:T(8,128)S(1)}) custom-call(s32[1]{0:T(128)S(6)} %copy.9.len_ref, bf16[128,2048]{1,0:T(8,128)(2,1)S(1)} %bitcast.7, bf16[64,4096]{1,0:T(8,128)(2,1)S(1)} %bitcast.8, bf16[128,2048]{1,0:T(8,128)(2,1)S(1)} %bitcast.9, bf16[256,4096]{1,0:T(8,128)(2,1)S(1)} %bitcast.5), custom_call_target="tpu_custom_call" | custom-call | tf_op jit(solution)/shard_map/pallas_call | solution.py:321
  71.5 0.8 %copy.10 = bf16[1,128,2048]{2,1,0:T(8,128)(2,1)} copy(bf16[1,128,2048]{2,1,0:T(8,128)(2,1)S(1)} %bitcast.6) | data formatting | bytes 1048576
  72.3 0.6 copy.11
Async XLA Ops:
  1.3 1.6 %copy-start = (bf16[1,256,4096]{2,1,0:T(8,128)(2,1)S(1)}, bf16[1,256,4096]{2,1,0:T(8,128)(2,1)}, u32[]{:S(2)}) copy-start(bf16[1,256,4096]{2,1,0:T(8,128)(2,1)} %param.8) | copy-start | bytes 6291460
  2.9 1.0 %copy-start.1 = (bf16[1,128,2048]{2,1,0:T(8,128)(2,1)S(1)}, bf16[1,128,2048]{2,1,0:T(8,128)(2,1)}, u32[]{:S(2)}) copy-start(bf16[1,128,2048]{2,1,0:T(8,128)(2,1)} %param.5) | copy-start | bytes 1572868
  3.9 1.0 %copy-start.2 = (bf16[1,64,4096]{2,1,0:T(8,128)(2,1)S(1)}, bf16[1,64,4096]{2,1,0:T(8,128)(2,1)}, u32[]{:S(2)}) copy-start(bf16[1,64,4096]{2,1,0:T(8,128)(2,1)} %param.6) | copy-start | bytes 1572868
  5.0 1.0 %copy-start.3 = (bf16[1,128,2048]{2,1,0:T(8,128)(2,1)S(1)}, bf16[1,128,2048]{2,1,0:T(8,128)(2,1)}, u32[]{:S(2)}) copy-start(bf16[1,128,2048]{2,1,0:T(8,128)(2,1)} %param.7) | copy-start | bytes 1572868

commit v2 on v1

--- a/solution.py
+++ b/solution.py
@@ -33,9 +33,9 @@
 
 
 def kernel(
-    len_ref, q_ref, kv_ref, do_ref, w_ref, dq_ref, eg_ref,
-    g, xs, wv, asend, abuf, bsend, bbuf,
-    wl_sem, ws_sem, wr_sem, xs_sem, xr_sem, zs_sem, zr_sem, as_sem, ar_sem, bs_sem, br_sem,
+    len_in, q_in, kv_in, do_in, w_ref, dq_ref, eg_ref,
+    q_ref, kv_ref, do_ref, g, xs, wv, asend, abuf, bsend, bbuf, len_ref,
+    len_sem, in_sem, wl_sem, ws_sem, wr_sem, xs_sem, xr_sem, zs_sem, zr_sem, as_sem, ar_sem, bs_sem, br_sem,
 ):
     section, dp = lax.axis_index("section"), lax.axis_index("dp")
     y, xl, c = section // 4, (section // 2) % 2, section % 2
@@ -46,6 +46,15 @@
 
     def around(k):
         return device(y, (xl + k // 4) % 2, (c + (k // 2) % 2) % 2, z, (xh + k % 2) % 2)
+
+    def load(half):
+        copies = []
+        for which, (source, place, part) in enumerate(
+            ((q_in, q_ref, 0), (kv_in, kv_ref, 0), (kv_in, kv_ref, 1), (do_in, do_ref, 0))
+        ):
+            cols = pl.ds(pl.multiple_of(part * WIDTH + (xh if half == 0 else 1 - xh) * (HALF * HD), HD), HALF * HD)
+            copies.append(pltpu.make_async_copy(source.at[:, cols], place.at[:, cols], in_sem.at[half, which]))
+        return copies
 
     barrier = pltpu.get_barrier_semaphore()
     for up in (1, RING - 1):
@@ -53,6 +62,12 @@
     for k in range(1, 8):
         pl.semaphore_signal(barrier, inc=1, device_id=around(k), device_id_type=MESH)
         pl.semaphore_signal(barrier, inc=1, device_id=device((y + k) % RING, xl, c, z, xh), device_id_type=MESH)
+
+    len_copy = pltpu.make_async_copy(len_in, len_ref, len_sem)
+    len_copy.start()
+    for half in range(2):
+        for copy in load(half):
+            copy.start()
 
     def w_columns(half, hh, part):
         return pl.ds(pl.multiple_of(part * WIDTH + (half * HALF + hh) * HD, HD), HD)
@@ -100,6 +115,7 @@
             device_id_type=MESH,
         )
 
+    len_copy.wait()
     live = lax.broadcasted_iota(jnp.int32, (SENC, TDEC), 0) < len_ref[0]
 
     def head(index):
@@ -118,26 +134,35 @@
         dv = dot_nn(probs_low, do).astype(BF)
         return dk, dv
 
-    def pair(hh):
+    def own_head(hh):
         dk, dv = head(xh * HALF + hh)
         g[0, hh, :SENC, :HD] = dk
         g[0, hh, :SENC, HD:] = dv
+
+    def other_head(hh):
         dk, dv = head((1 - xh) * HALF + hh)
         xs[hh, :, :HD] = dk
         xs[hh, :, HD:] = dv
 
-    def send_pair(hh):
+    def send_own(hh):
         z_copy(1, 0, 0, hh).start()
         z_copy(1, 1, 0, hh).start()
+
+    for copy in load(0):
+        copy.wait()
+    own_head(0)
+    for copy in load(1):
+        copy.wait()
+    other_head(0)
+    pl.semaphore_wait(barrier, 16)
+    send_own(0)
+    x_copy(0).start()
+
+    def more(hh, _):
+        own_head(hh)
+        send_own(hh)
+        other_head(hh)
         x_copy(hh).start()
-
-    pair(0)
-    pl.semaphore_wait(barrier, 16)
-    send_pair(0)
-
-    def more(hh, _):
-        pair(hh)
-        send_pair(hh)
         return 0
 
     lax.fori_loop(1, HALF, more, 0)
@@ -186,8 +211,7 @@
                     at = d * 64 + j * 32
                     asend[group, r * 4 + j * 2 + n, d * 32 : d * 32 + 32, :] = total[at : at + 32, n * HD : n * HD + HD]
 
-    def product_edge(t, group):
-        total = product(t)
+    def place_edge(total, group):
         for r in range(2):
             for j in range(2):
                 for n in range(2):
@@ -231,6 +255,7 @@
         for k in range(1, 8):
             a_copy(group, k).wait_recv()
             total += abuf[group, k, :rows, :].astype(F32)
+        total = total.astype(BF)
         bsend[group, :rows, :] = total
         for d in range(rows // 32):
             away = b_place(group, d) != y
@@ -256,24 +281,17 @@
     lax.fori_loop(2, 4, step_a, 0)
     a_start(2)
     last_hop(1, 0)
-    product_edge(0, 0)
+    last_hop(1, 1)
+    place_edge(product(0), 0)
+    last_hop(1, 2)
+    last_hop(1, 3)
     a_start(0)
-    last_hop(1, 1)
     product_ring(5)
-    last_hop(1, 2)
-    gather_sum(1)
-    last_hop(1, 3)
     product_ring(6)
     a_start(3)
+    gather_sum(1)
     gather_sum(2)
     gather_sum(0)
-
-    for r in range(2):
-        lax.fori_loop(0, HALF, lambda hh, _, r=r: (z_copy(4, r, r, hh).wait_recv(), 0)[1], 0)
-    product_edge(7, 4)
-    a_start(4)
-    gather_sum(3)
-    gather_sum(4)
 
     for hh in range(HALF):
         x_copy(hh).wait_send()
@@ -285,19 +303,41 @@
             for d in range(2):
                 for r in range(2):
                     z_copy(s, d, r, hh).wait_send()
-        for r in range(2):
-            z_copy(4, r, r, hh).wait_send()
         return 0
 
     lax.fori_loop(0, HALF, sent, 0)
-    for group in range(5):
+
+    def a_sent(group):
         for k in range(1, 8):
             a_copy(group, k).wait_send()
+
+    def b_sent(group):
         for d in range(1 if group in (0, 4) else 2):
 
             @pl.when(b_place(group, d) != y)
             def _():
                 b_copy(group, d).wait_send()
+
+    for group in range(3):
+        a_sent(group)
+        b_sent(group)
+
+    far = None
+    for hh in range(HALF):
+        for r in range(2):
+            z_copy(4, r, r, hh).wait_recv()
+        part = dot_nt(g[7, hh], wv[hh])
+        far = part if far is None else far + part
+    place_edge(far.astype(BF), 4)
+    a_start(4)
+    gather_sum(3)
+    for hh in range(HALF):
+        for r in range(2):
+            z_copy(4, r, r, hh).wait_send()
+    gather_sum(4)
+    for group in (3, 4):
+        a_sent(group)
+        b_sent(group)
 
     for k in range(1, RING):
         other = (y + k) % RING
@@ -309,14 +349,15 @@
             device_id=device(other, xl, c, z, xh),
             device_id_type=MESH,
         ).wait_recv()
-    total = bbuf[0]
+    total = bbuf[0].astype(F32)
     for k in range(1, RING):
-        total += bbuf[k]
+        total += bbuf[k].astype(F32)
     eg_ref[...] = total
 
 
 def local(queries, key_values, d_context, w_kv, enc_len):
     vmem = pl.BlockSpec(memory_space=pltpu.VMEM)
+    anywhere = pl.BlockSpec(memory_space=pl.ANY)
     dma = pltpu.SemaphoreType.DMA
     dquery, encoder_grad = pl.pallas_call(
         kernel,
@@ -324,24 +365,28 @@
             jax.ShapeDtypeStruct((TDEC, WIDTH), BF),
             jax.ShapeDtypeStruct((32, HD), F32),
         ),
-        in_specs=[pl.BlockSpec(memory_space=pltpu.SMEM), vmem, vmem, vmem, pl.BlockSpec(memory_space=pl.ANY)],
+        in_specs=[anywhere, anywhere, anywhere, anywhere, anywhere],
         out_specs=(vmem, vmem),
         scratch_shapes=[
+            pltpu.VMEM((TDEC, WIDTH), BF),
+            pltpu.VMEM((SENC, 2 * WIDTH), BF),
+            pltpu.VMEM((TDEC, WIDTH), BF),
             pltpu.VMEM((8, HALF, 2 * SENC, 2 * HD), BF),
             pltpu.VMEM((HALF, SENC, 2 * HD), BF),
             pltpu.VMEM((HALF, 2 * HD, 2 * HD), BF),
             pltpu.VMEM((5, 8, 64, HD), BF),
             pltpu.VMEM((5, 8, 64, HD), BF),
-            pltpu.VMEM((5, 64, HD), F32),
-            pltpu.VMEM((RING, 32, HD), F32),
-            dma((HALF, 2)), dma((HALF, 2)), dma((HALF, 2)),
+            pltpu.VMEM((5, 64, HD), BF),
+            pltpu.VMEM((RING, 32, HD), BF),
+            pltpu.SMEM((1,), jnp.int32),
+            dma, dma((2, 4)), dma((HALF, 2)), dma((HALF, 2)), dma((HALF, 2)),
             dma((HALF,)), dma((HALF,)),
             dma((4, 2, 2, HALF)), dma((4, 2, 2, HALF)),
             dma((5, 8)), dma((5, 8)),
             dma((5, 2)), dma((RING,)),
         ],
         compiler_params=pltpu.CompilerParams(
-            collective_id=0, has_side_effects=True, vmem_limit_bytes=40 * 1024 * 1024
+            collective_id=0, has_side_effects=True, vmem_limit_bytes=54400 * 1024
         ),
     )(enc_len, queries[0], key_values[0], d_context[0], w_kv[0])
     return dquery[None], encoder_grad

time: 73.6 us -> 67.9 us (0.923)
  local copies, waits for them, and re-layouts: 6.12 us -> 1.41 us
    unnamed x10 -> x2, local copies, waits for them, and re-layouts: 6.12 us -> 1.41 us
where the time goes in v2:
time: 67.9 us; the launch traced here: 67.6 us
  Pallas kernels  64.9 us (96%)
  local copies, waits for them, and re-layouts  1.41 us (2%)
  between operations  1.29 us (2%)
    pallas_call x1, Pallas kernels, local(): pl.pallas_call(kernel, out_shape=(jax.ShapeDtypeStruct((TDEC, WIDTH), BF)...  64.9 us
    unnamed x2, local copies, waits for them, and re-layouts  1.41 us

profile of v2, /device:TPU:1, one launch (start us, length us, event | category | flops | bytes accessed | tf_op | source)
XLA Modules:
  0.0 67.6 jit_solution(13413798428663605749)
XLA Ops:
  1.3 64.9 %shard_map.68 = (bf16[128,2048]{1,0:T(8,128)(2,1)S(1)}, f32[32,256]{1,0:T(8,128)S(1)}) custom-call(s32[1]{0:T(128)S(6)} %copy.9.len_in, bf16[128,2048]{1,0:T(8,128)(2,1)} %bitcast.7, bf16[64,4096]{1,0:T(8,128)(2,1)} %bitcast.8, bf16[128,2048]{1,0:T(8,128)(2,1)} %bitcast.9, bf16[256,4096]{1,0:T(8,128)(2,1)} %bitcast.6), custom_call_target="tpu_custom_call" | custom-call | tf_op jit(solution)/shard_map/pallas_call | solution.py:362
  66.2 0.8 %copy.10 = bf16[1,128,2048]{2,1,0:T(8,128)(2,1)} copy(bf16[1,128,2048]{2,1,0:T(8,128)(2,1)S(1)} %bitcast.5) | data formatting | bytes 1048576
  67.0 0.6 copy.11

commit v3 on v2

--- a/solution.py
+++ b/solution.py
@@ -233,7 +233,7 @@
         )
 
     def a_start(group):
-        for k in range(1, 8):
+        for k in (1, 5, 3, 7, 4, 6, 2):
             a_copy(group, k).start()
 
     def b_place(group, d):
@@ -331,10 +331,10 @@
     place_edge(far.astype(BF), 4)
     a_start(4)
     gather_sum(3)
+    gather_sum(4)
     for hh in range(HALF):
         for r in range(2):
             z_copy(4, r, r, hh).wait_send()
-    gather_sum(4)
     for group in (3, 4):
         a_sent(group)
         b_sent(group)
@@ -353,6 +353,15 @@
     for k in range(1, RING):
         total += bbuf[k].astype(F32)
     eg_ref[...] = total
+
+
+def write_out(dq_ref, eg_ref, dq_out, eg_out, dq_sem, eg_sem):
+    dq_copy = pltpu.make_async_copy(dq_ref, dq_out, dq_sem)
+    eg_copy = pltpu.make_async_copy(eg_ref, eg_out, eg_sem)
+    dq_copy.start()
+    eg_copy.start()
+    dq_copy.wait()
+    eg_copy.wait()
 
 
 def local(queries, key_values, d_context, w_kv, enc_len):
@@ -389,6 +398,17 @@
             collective_id=0, has_side_effects=True, vmem_limit_bytes=54400 * 1024
         ),
     )(enc_len, queries[0], key_values[0], d_context[0], w_kv[0])
+    dquery, encoder_grad = pl.pallas_call(
+        write_out,
+        out_shape=(
+            jax.ShapeDtypeStruct((TDEC, WIDTH), BF),
+            jax.ShapeDtypeStruct((32, HD), F32),
+        ),
+        in_specs=[vmem, vmem],
+        out_specs=(anywhere, anywhere),
+        scratch_shapes=[dma, dma],
+        compiler_params=pltpu.CompilerParams(vmem_limit_bytes=54400 * 1024),
+    )(dquery, encoder_grad)
     return dquery[None], encoder_grad
 
 

time: 67.9 us -> 67.3 us (level)
  local copies, waits for them, and re-layouts: 1.41 us -> 0 us
  Pallas kernels: 64.9 us -> 65.7 us
    unnamed x2 -> x0, local copies, waits for them, and re-layouts: 1.41 us -> none
    pallas_call x0 -> x1, Pallas kernels: none -> 0.81 us  [local(): pl.pallas_call(write_out, out_shape=(jax.ShapeDtypeStruct((TDEC, WIDTH),...]
where the time goes in v3:
time: 67.3 us; the launch traced here: 67 us
  Pallas kernels  65.7 us (98%)
  between operations  1.29 us (2%)
    pallas_call x1, Pallas kernels, local(): pl.pallas_call(kernel, out_shape=(jax.ShapeDtypeStruct((TDEC, WIDTH), BF)...  64.9 us

profile of v3, /device:TPU:1, one launch (start us, length us, event | category | flops | bytes accessed | tf_op | source)
XLA Modules:
  0.0 67.0 jit_solution(4577940001997036040)
XLA Ops:
  1.3 64.9 %shard_map.68 = (bf16[128,2048]{1,0:T(8,128)(2,1)S(1)}, f32[32,256]{1,0:T(8,128)S(1)}) custom-call(s32[1]{0:T(128)S(6)} %copy.7.len_in, bf16[128,2048]{1,0:T(8,128)(2,1)} %bitcast.6, bf16[64,4096]{1,0:T(8,128)(2,1)} %bitcast.7, bf16[128,2048]{1,0:T(8,128)(2,1)} %bitcast.8, bf16[256,4096]{1,0:T(8,128)(2,1)} %bitcast.5), custom_call_target="tpu_custom_call" | custom-call | tf_op jit(solution)/shard_map/pallas_call | solution.py:371
  66.2 0.8 %shard_map.69 = (bf16[128,2048]{1,0:T(8,128)(2,1)}, f32[32,256]{1,0:T(8,128)}) custom-call(bf16[128,2048]{1,0:T(8,128)(2,1)S(1)} %get-tuple-element.6.dq_ref, f32[32,256]{1,0:T(8,128)S(1)} %get-tuple-element.7.eg_ref), custom_call_target="tpu_custom_call" | custom-call | tf_op jit(solution)/shard_map/pallas_call | solution.py:401
